TPU v7x, 32 devices: a whole 2x2x4 slice. The times are simulated.
32 devices in a mesh: grp: 4 (over x, core), blk: 8 (over z, y).
Axes of the slice: x: 2, y: 2, z: 4, core: 2. Of those that a mesh axis runs over, the one named last changes fastest.
Arguments:
- integrals: bfloat16 [8192, 32768], P('blk', 'grp'), may hold values from -0.046875 to 0.046875
- block_mask: int32 [64, 256], P('blk', 'grp'), may hold values from 0 to 1, as said below
- amplitudes: bfloat16 [32768, 1024], P(('grp', 'blk')), may hold values from -6 to 6
- pair_batches: int32 [8], replicated, may hold values from 0 to 7, each once
Outputs:
- ladder: bfloat16 [1024, 8192], P('grp', 'blk')
Inputs may be any that keep to these rules, and one draw needn't show every extreme that they name: `block_mask`: 0 or 1; the share of kept tiles rises from about a quarter in the first tile row to about three quarters in the last. `pair_batches`: each batch number once.
All inputs are finite; a program needn't handle non-finite values.
Results may differ from a plain program's by a relative error of at most 0.001.
Values may be sent and summed in bfloat16 or wider, within the bound.
A program may use at most 128 MiB of HBM per device.

v0:
```python
import jax
import jax.numpy as jnp
from jax import lax
from jax.sharding import PartitionSpec as P

BLOCK = 128
BATCH = 128
NB = 8


def on_device(integrals, block_mask, amplitudes, pair_batches):
    rows_in = amplitudes.shape[0]
    grouped = amplitudes.reshape(rows_in, NB, BATCH)
    selector = (pair_batches[:, None] == jnp.arange(NB, dtype=jnp.int32)[None, :]).astype(
        jnp.bfloat16
    )
    picked = jnp.einsum("rnb,mn->rmb", grouped, selector, preferred_element_type=jnp.float32)
    chosen = picked.astype(jnp.bfloat16).reshape(rows_in, NB * BATCH)
    out_rows = integrals.shape[0]
    fragment = lax.all_gather(chosen, "blk", axis=0, tiled=True)
    number = fragment.shape[0]
    mcols = block_mask.astype(jnp.bfloat16)
    tiled = (
        integrals.reshape(out_rows // BLOCK, BLOCK, number // BLOCK, BLOCK)
        * mcols[:, None, :, None]
    )
    masked = tiled.reshape(out_rows, number)
    partial_sum = lax.dot_general(
        fragment, masked, (((0,), (1,)), ((), ())), preferred_element_type=jnp.float32
    )
    owned = lax.psum_scatter(partial_sum, "grp", scatter_dimension=0, tiled=True)
    return owned.astype(jnp.bfloat16)


def solution(mesh):
    in_specs = (P("blk", "grp"), P("blk", "grp"), P(("grp", "blk"), None), P())
    out_specs = P("grp", "blk")
    return jax.shard_map(
        on_device, mesh=mesh, in_specs=in_specs, out_specs=out_specs, check_vma=False
    )
```

profile of v0, /device:TPU:1, one launch (start us, length us, event | category | flops | bytes accessed | tf_op | source)
XLA Modules:
  0.0 329.8 jit_solution(16754064573178667119)
XLA Ops:
  6.5 0.0 all-gather.2.cloned.1.call-start
  6.5 2.2 copy.5
  8.8 1.4 convolution_convert_fusion
  10.2 2.0 copy.13
  12.1 0.0 all-gather.2.cloned.1.call-update
  12.2 0.0 reduce-scatter.2.cloned.1.call-start
  12.2 0.7 convert_element_type.15
  12.9 228.7 %all-gather.2.cloned.1.call-done = bf16[8192,1024]{1,0:T(8,128)(2,1)} async-done(((bf16[1024,1024]{1,0:T(8,128)(2,1)}), bf16[8192,1024]{1,0:T(8,128)(2,1)}) %all-gather.2.cloned.1.call-update) | async-done | bytes 16777232 | tf_op jit(solution)/shard_map/all_gather | solution.py:20
  241.6 6.5 %mul.11 = bf16[8,128,64,128]{3,2,1,0:T(8,128)(2,1)} broadcast(bf16[8,64]{1,0:T(8,128)(2,1)S(1)} %convert_element_type.15), dimensions={0,2} | broadcast | bytes 16778240 | tf_op jit(solution)/shard_map/mul | solution.py:24
  248.1 29.5 %fusion = f32[1024,1024]{1,0:T(8,128)} fusion(bf16[8192,1024]{1,0:T(8,128)(2,1)} %all-gather.2.cloned.1.call-done, bf16[1024,8192]{1,0:T(8,128)(2,1)} %param.4, bf16[128,8,64,128]{3,2,1,0:T(8,128)(2,1)} %bitcast.17), kind=kOutput, calls=%fused_computation.1 | convolution fusion | flops 17188257792 | bytes 54525952 | tf_op jit(solution)/shard_map/dot_general | solution.py:28
  277.6 0.0 reduce-scatter.2.cloned.1.call-update
  277.6 43.2 %reduce-scatter.2.cloned.1.call-done = f32[256,1024]{1,0:T(8,128)} async-done(((f32[1024,1024]{1,0:T(8,128)}), f32[256,1024]{1,0:T(8,128)}) %reduce-scatter.2.cloned.1.call-update) | async-done | bytes 1048592 | tf_op jit(solution)/shard_map/reduce_scatter | solution.py:31
  320.8 2.1 convert_element_type.16
Async XLA Ops:
  6.5 235.1 %all-gather.2.cloned.1.call-start = ((), (), s32[]{:S(2)}) async-start(), calls=%async_computation.1 | async-start | bytes 18874368 | tf_op jit(solution)/shard_map/all_gather | solution.py:20
  12.2 308.7 %reduce-scatter.2.cloned.1.call-start = ((), (), s32[]{:S(2)}) async-start(), calls=%async_computation.2 | async-start | bytes 5242880 | tf_op jit(solution)/shard_map/reduce_scatter | solution.py:31
Sparse Core Ops, SparseCore 0:
  12.3 229.2 all-gather.1
  277.7 43.0 reduce-scatter.1
where the time goes:
time: 331 us; the launch traced here: 330 us
  waiting for transfers between devices  272 us (82%)
  matrix products  30.9 us (9%)
  between operations  13.4 us (4%)
  local copies, waits for them, and re-layouts  10.6 us (3%)
    all_gather x1, waiting for transfers between devices, on_device(): fragment = lax.all_gather(chosen, 'blk', axis=0, tiled=True)  229 us
    reduce_scatter x1, waiting for transfers between devices, on_device(): lax.psum_scatter(partial_sum, 'grp', scatter_dimension=0, tiled=True)  43.2 us
    dot_general x1, matrix products, on_device(): lax.dot_general(fragment, masked, (((0,), (1,)), ((), ())), preferred_ele...  29.5 us
  transfers between devices with their start and end apart: 2, of which 2 were waited for; matrix products, arithmetic and copies ran while one was open for 0% of the time, Pallas kernels for 0%

commit v1 on v0

v1 whole, which is shorter than its diff:
```python
import functools

import jax
import jax.numpy as jnp
from jax import lax
from jax.experimental import pallas as pl
from jax.experimental.pallas import tpu as pltpu
from jax.sharding import PartitionSpec as P

BLOCK = 128
BATCH = 128
NB = 8
LAG = 2
MESH = pl.DeviceIdType.MESH


def plain(integrals, block_mask, amplitudes, pair_batches):
    rows_in = amplitudes.shape[0]
    grouped = amplitudes.reshape(rows_in, NB, BATCH)
    chosen = jnp.take(grouped, pair_batches, axis=1).reshape(rows_in, NB * BATCH)
    out_rows = integrals.shape[0]
    fragment = lax.all_gather(chosen, "blk", axis=0, tiled=True)
    number = fragment.shape[0]
    mcols = block_mask.astype(jnp.bfloat16)
    tiled = (
        integrals.reshape(out_rows // BLOCK, BLOCK, number // BLOCK, BLOCK)
        * mcols[:, None, :, None]
    )
    masked = tiled.reshape(out_rows, number)
    partial_sum = lax.dot_general(
        fragment, masked, (((0,), (1,)), ((), ())), preferred_element_type=jnp.float32
    )
    owned = lax.psum_scatter(partial_sum, "grp", scatter_dimension=0, tiled=True)
    return owned.astype(jnp.bfloat16)


def kernel(
    nz, beta,
    mask_ref, amp_ref, int_ref, out_ref,
    T, V, acc, sib, far,
    v_sem, zfs, zbs, zfr, zbr, yas, yar, ybs, ybr, sibs, sibr, fars, farr,
):
    g, b = lax.axis_index("grp"), lax.axis_index("blk")
    x, c = g // 2, g % 2
    z, y = b // 2, b % 2
    Q, nb, R, _ = T.shape
    pairs = Q // 2
    rows_out = V.shape[0]
    alpha = R - beta
    has_l, has_r = z > 0, z < nz - 1
    sibling = (x * 2 + 1 - c, b)
    opposite = ((1 - x) * 2 + c, b)
    partner = (g, z * 2 + 1 - y)
    toward = ((g, jnp.minimum(z + 1, nz - 1) * 2 + y), (g, jnp.maximum(z - 1, 0) * 2 + y))

    def remote(src, dst, send, recv, device):
        return pltpu.make_async_remote_copy(
            src_ref=src, dst_ref=dst, send_sem=send, recv_sem=recv,
            device_id=device, device_id_type=MESH,
        )

    def z_full(q, o, d):
        ref = T.at[q, 2 * o + y]
        return remote(ref, ref, zfs.at[q, d, o], zfr.at[q, o], toward[d])

    def z_part(q, o, d):
        ref = T.at[q, 2 * o + 1 - y, pl.ds(alpha, beta)]
        return remote(ref, ref, zbs.at[q, d, o], zbr.at[q, o], toward[d])

    def y_first(q, o, v):
        ref = T.at[q, 2 * o + v, pl.ds(0, alpha)]
        return remote(ref, ref, yas.at[q, o], yar.at[q, o], partner)

    def y_last(q, v):
        ref = T.at[q, 2 * z + v, pl.ds(alpha, beta)]
        return remote(ref, ref, ybs.at[q], ybr.at[q], partner)

    def to_sibling(q, j):
        return remote(acc.at[q], sib.at[j], sibs.at[j], sibr.at[j], sibling)

    def to_opposite(q, j):
        return remote(acc.at[q, 1 - x], far.at[j], fars.at[j], farr.at[j], opposite)

    load_v = pltpu.make_async_copy(int_ref, V, v_sem)
    load_v.start()

    barrier = pltpu.get_barrier_semaphore()
    for device in (sibling, opposite, partner):
        pl.semaphore_signal(barrier, inc=1, device_id=device, device_id_type=MESH)
    for d, there in ((0, has_r), (1, has_l)):
        @pl.when(there)
        def _():
            pl.semaphore_signal(barrier, inc=1, device_id=toward[d], device_id_type=MESH)

    def choose(q):
        for half in range(2):
            k = (NB // 2) * half + (NB // 4) * (q % 2) + q // 2
            T[q, b, :, half * BATCH:(half + 1) * BATCH] = amp_ref[:, k * BATCH:(k + 1) * BATCH]

    choose(0)
    choose(1)
    pl.semaphore_wait(barrier, 3 + has_r.astype(jnp.int32) + has_l.astype(jnp.int32))

    def gemm(q, shard):
        tile = min(256, rows_out)

        def rows_of(i, _):
            rows = pl.ds(pl.multiple_of(i * tile, tile), tile)
            cols = pl.ds(pl.multiple_of(shard * R, 128), R)
            res = jnp.dot(V[rows, cols], T[q, shard], preferred_element_type=jnp.float32)
            acc[q, 0, rows, :] += res[:, :BATCH]
            acc[q, 1, rows, :] += res[:, BATCH:]
            return 0

        lax.fori_loop(0, rows_out // tile, rows_of, 0)

    def start_own(p):
        for qi in range(2):
            q = 2 * p + qi
            y_last(q, y).start()
            for d, there in ((0, has_r), (1, has_l)):
                @pl.when(there)
                def _():
                    z_full(q, z, d).start()
            y_first(q, z, y).start()
        for qi in range(2):
            q = 2 * p + qi
            y_last(q, 1 - y).wait_recv()
            for d, there in ((0, has_r), (1, has_l)):
                @pl.when(there)
                def _():
                    z_part(q, z, d).start()

    def forward(p, s):
        for qi in range(2):
            q = 2 * p + qi
            for d, there in ((0, has_r), (1, has_l)):
                o = z - s if d == 0 else z + s

                @pl.when((o >= 0) & (o < nz))
                def _():
                    z_full(q, o, d).wait_recv()

                    @pl.when(there)
                    def _():
                        z_full(q, o, d).start()

                    y_first(q, o, y).start()
                    z_part(q, o, d).wait_recv()

                    @pl.when(there)
                    def _():
                        z_part(q, o, d).start()

    def each(p, s, act):
        def one(i, _):
            q, d = 2 * p + i // 2, i % 2
            o = z + s * (2 * d - 1)

            @pl.when((o >= 0) & (o < nz) & ((d == 0) | (s > 0)))
            def _():
                act(q, o)
            return 0

        lax.fori_loop(0, 4, one, 0)

    def lagged(q, o):
        y_first(q, o, 1 - y).wait_recv()
        gemm(q, 2 * o + 1 - y)

    def reduce_a(p):
        for qi in range(2):
            @pl.when(c != qi)
            def _():
                to_sibling(2 * p + qi, p).start()

    def reduce_b(p):
        q = 2 * p + c
        to_sibling(q, p).wait_recv()
        acc[q, 1 - x] += sib[p, 1 - x]
        to_opposite(q, p).start()
        acc[q, x] += sib[p, x]

    def reduce_c(p):
        q = 2 * p + c
        to_opposite(q, p).wait_recv()

        def cols(i, _):
            rows = pl.ds(pl.multiple_of(i * BLOCK, BLOCK), BLOCK)
            total = acc[q, x, rows, :] + far[p, rows, :]
            out_ref[pl.ds(pl.multiple_of(p * BATCH, BATCH), BATCH), rows] = total.T.astype(jnp.bfloat16)
            return 0

        lax.fori_loop(0, rows_out // BLOCK, cols, 0)

    def mask_tiles():
        def tile(i, _):
            r, k = i // (V.shape[1] // BLOCK), i % (V.shape[1] // BLOCK)
            at = (
                pl.ds(pl.multiple_of(r * BLOCK, BLOCK), BLOCK),
                pl.ds(pl.multiple_of(k * BLOCK, BLOCK), BLOCK),
            )
            keep = jnp.full((BLOCK, BLOCK), mask_ref[r, k].astype(jnp.float32)).astype(jnp.bfloat16)
            V[at] = V[at] * keep
            return 0

        lax.fori_loop(0, (rows_out // BLOCK) * (V.shape[1] // BLOCK), tile, 0)

    def step(t, _):
        p, s = t // nz, t % nz

        @pl.when(t < pairs * nz)
        def _():
            @pl.when(s == 0)
            def _():
                start_own(p)

            @pl.when(s > 0)
            def _():
                forward(p, s)

            @pl.when(t == 0)
            def _():
                for q in range(2, Q):
                    choose(q)
                acc[...] = jnp.zeros_like(acc)
                load_v.wait()
                mask_tiles()

            each(p, s, lambda q, o: gemm(q, 2 * o + y))

        @pl.when(t >= LAG)
        def _():
            late = jnp.maximum(t - LAG, 0)
            each(late // nz, late % nz, lagged)

        done = p - 1
        for at, act in ((LAG - 1, reduce_a), (LAG, reduce_b), (LAG + 1, reduce_c)):
            @pl.when((done >= 0) & (done < pairs - 1) & (s == at))
            def _():
                act(done)
        return 0

    lax.fori_loop(0, pairs * nz + LAG, step, 0)
    for act in (reduce_a, reduce_b, reduce_c):
        act(pairs - 1)

    def drain(i, _):
        q, o = i // nz, i % nz

        @pl.when((o <= z) & has_r)
        def _():
            z_full(q, o, 0).wait_send()
            z_part(q, o, 0).wait_send()

        @pl.when((o >= z) & has_l)
        def _():
            z_full(q, o, 1).wait_send()
            z_part(q, o, 1).wait_send()

        y_first(q, o, y).wait_send()
        return 0

    lax.fori_loop(0, Q * nz, drain, 0)
    for q in range(Q):
        y_last(q, y).wait_send()
    for p in range(pairs):
        to_sibling(2 * p + 1 - c, p).wait_send()
        to_opposite(2 * p + c, p).wait_send()


def fused(nb, integrals, block_mask, amplitudes, pair_batches):
    rows_out, number = integrals.shape
    R, occ = amplitudes.shape
    Q, nz = NB // 2, nb // 2
    beta = max(16, R // 6 // 16 * 16)
    chosen = jnp.take(amplitudes.reshape(R, NB, BATCH), pair_batches, axis=1).reshape(R, occ)
    dma = pltpu.SemaphoreType.DMA
    return pl.pallas_call(
        functools.partial(kernel, nz, beta),
        out_shape=jax.ShapeDtypeStruct((occ // 4, rows_out), jnp.bfloat16),
        in_specs=[
            pl.BlockSpec(memory_space=pltpu.SMEM),
            pl.BlockSpec(memory_space=pltpu.VMEM),
            pl.BlockSpec(memory_space=pl.ANY),
        ],
        out_specs=pl.BlockSpec(memory_space=pltpu.VMEM),
        scratch_shapes=[
            pltpu.VMEM((Q, nb, R, 2 * BATCH), jnp.bfloat16),
            pltpu.VMEM((rows_out, number), jnp.bfloat16),
            pltpu.VMEM((Q, 2, rows_out, BATCH), jnp.float32),
            pltpu.VMEM((Q // 2, 2, rows_out, BATCH), jnp.float32),
            pltpu.VMEM((Q // 2, rows_out, BATCH), jnp.float32),
            dma,
            dma((Q, 2, nz)), dma((Q, 2, nz)), dma((Q, nz)), dma((Q, nz)),
            dma((Q, nz)), dma((Q, nz)), dma((Q,)), dma((Q,)),
            dma((Q // 2,)), dma((Q // 2,)), dma((Q // 2,)), dma((Q // 2,)),
        ],
        compiler_params=pltpu.CompilerParams(
            collective_id=0, has_side_effects=True, vmem_limit_bytes=56 * 2**20
        ),
        cost_estimate=pl.CostEstimate(
            flops=2 * occ * rows_out * number,
            bytes_accessed=2 * rows_out * number + 2 * nb * R * occ,
            transcendentals=0,
        ),
    )(block_mask, chosen, integrals)


def solution(mesh):
    ng, nb = mesh.shape["grp"], mesh.shape["blk"]
    takes = ng == 4 and nb % 2 == 0 and nb // 2 >= LAG + 2
    in_specs = (P("blk", "grp"), P("blk", "grp"), P(("grp", "blk"), None), P())
    return jax.shard_map(
        functools.partial(fused, nb) if takes else plain,
        mesh=mesh, in_specs=in_specs, out_specs=P("grp", "blk"), check_vma=False,
    )
```

time: 331 us -> 205 us (0.62)
  waiting for transfers between devices: 272 us -> 0 us
  Pallas kernels: 0 us -> 193 us
  matrix products: 30.9 us -> 0 us
  between operations: 13.4 us -> 0.04 us
    all_gather x1 -> x0, waiting for transfers between devices: 229 us -> none  [on_device(): fragment = lax.all_gather(chosen, 'blk', axis=0, tiled=True)]
    pallas_call x0 -> x1, Pallas kernels: none -> 193 us  [fused(): pl.pallas_call(functools.partial(kernel, nz, beta), out_shape=jax.ShapeDt...]
    reduce_scatter x1 -> x0, waiting for transfers between devices: 43.2 us -> none  [on_device(): lax.psum_scatter(partial_sum, 'grp', scatter_dimension=0, tiled=True)]
    dot_general x2 -> x0, matrix products: 30.9 us -> none  [the longest x1 29.5 us: on_device(): lax.dot_general(fragment, masked, (((0,), (1,)), ((), ())), preferred_ele...]
    mul x1 -> x0, local copies, waits for them, and re-layouts: 6.47 us -> none  [on_device(): integrals.reshape(out_rows // BLOCK, BLOCK, number // BLOCK, BLOCK)]
  transfers between devices with their start and end apart: 2 -> 0, of which waited for: 2 -> 0; matrix products, arithmetic and copies ran while one was open for 0% -> 0% of each run, Pallas kernels for 0% -> 0%
where the time goes in v1:
time: 205 us
  Pallas kernels  193 us (94%)
  local copies, waits for them, and re-layouts  9.74 us (5%)
    pallas_call x1, Pallas kernels, fused(): pl.pallas_call(functools.partial(kernel, nz, beta), out_shape=jax.ShapeDt...  193 us
    unnamed x4, local copies, waits for them, and re-layouts  4.73 us

profile of v1, /device:TPU:1, one launch (start us, length us, event | category | flops | bytes accessed | tf_op | source)
XLA Modules:
  0.0 204.7 jit_solution(1903148666990360253)
XLA Ops:
  0.0 2.9 %copy.6 = bf16[1024,1024]{0,1:T(8,128)(2,1)S(1)} copy(bf16[1024,1024]{1,0:T(8,128)(2,1)} %param.6) | data formatting | bytes 4194304 | tf_op args[2]
  2.9 0.0 copy-start
  2.9 2.4 %copy.7 = bf16[1024,8,128]{2,0,1:T(8,128)(2,1)} copy(bf16[1024,8,128]{0,2,1:T(8,128)(2,1)S(1)} %bitcast.9) | data formatting | bytes 4194304 | tf_op jit(solution)/shard_map/reshape | solution.py:277
  5.3 0.0 copy-done
  5.3 2.5 %gather_fusion = bf16[8,1024,128]{2,1,0:T(8,128)(2,1)S(1)} fusion(bf16[1024,8,128]{2,0,1:T(8,128)(2,1)} %copy.7, s32[1024]{0:T(1024)S(1)} %pad_clamp_fusion), kind=kCustom, calls=%fused_computation | custom fusion | bytes 4194336 | tf_op jit(solution)/shard_map/jit(_take)/gather | solution.py:277
  7.9 0.1 broadcast_bitcast_fusion
  7.9 1.8 bitcast_select_fusion.amp_ref
  9.8 193.0 %shard_map.46 = bf16[256,1024]{1,0:T(8,128)(2,1)} custom-call(s32[8,64]{1,0:T(8,128)} %mask_ref.1, bf16[1024,1024]{1,0:T(8,128)(2,1)} %bitcast_select_fusion.amp_ref, bf16[1024,8192]{1,0:T(8,128)(2,1)} %int_ref.1), custom_call_target="tpu_custom_call" | custom-call | flops 17179869184 | bytes 33554432 | tf_op jit(solution)/shard_map/pallas_call | solution.py:279
  202.8 1.9 copy.12
  (3 shorter events, 0.0 us)
Async XLA Ops:
  2.9 2.4 %copy-start = (s32[8]{0:T(128)S(1)}, s32[8]{0:T(128)}, u32[]{:S(2)}) copy-start(s32[8]{0:T(128)} %param.7) | copy-start | bytes 100

commit v2 on v1

--- a/solution.py
+++ b/solution.py
@@ -36,7 +36,7 @@
 
 def kernel(
     nz, beta,
-    mask_ref, amp_ref, int_ref, out_ref,
+    mask_ref, order_ref, amp_ref, int_ref, out_ref,
     T, V, acc, sib, far,
     v_sem, zfs, zbs, zfr, zbr, yas, yar, ybs, ybr, sibs, sibr, fars, farr,
 ):
@@ -75,8 +75,8 @@
         ref = T.at[q, 2 * z + v, pl.ds(alpha, beta)]
         return remote(ref, ref, ybs.at[q], ybr.at[q], partner)
 
-    def to_sibling(q, j):
-        return remote(acc.at[q], sib.at[j], sibs.at[j], sibr.at[j], sibling)
+    def to_sibling(q, j, h):
+        return remote(acc.at[q, h], sib.at[j, h], sibs.at[j, h], sibr.at[j, h], sibling)
 
     def to_opposite(q, j):
         return remote(acc.at[q, 1 - x], far.at[j], fars.at[j], farr.at[j], opposite)
@@ -95,7 +95,22 @@
     def choose(q):
         for half in range(2):
             k = (NB // 2) * half + (NB // 4) * (q % 2) + q // 2
-            T[q, b, :, half * BATCH:(half + 1) * BATCH] = amp_ref[:, k * BATCH:(k + 1) * BATCH]
+            picks = [
+                jnp.full((16, BATCH), jnp.where(order_ref[k] == n, 1.0, 0.0)).astype(jnp.bfloat16)
+                for n in range(NB)
+            ]
+
+            def some(i, _):
+                rows = pl.ds(pl.multiple_of(i * 128, 128), 128)
+                total = None
+                for n in range(NB):
+                    batch = amp_ref[rows, n * BATCH:(n + 1) * BATCH]
+                    term = batch * jnp.tile(picks[n], (8, 1))
+                    total = term if total is None else total + term
+                T[q, b, rows, half * BATCH:(half + 1) * BATCH] = total
+                return 0
+
+            lax.fori_loop(0, R // 128, some, 0)
 
     choose(0)
     choose(1)
@@ -103,6 +118,10 @@
 
     def gemm(q, shard):
         tile = min(256, rows_out)
+
+        @pl.when(q == 0)
+        def _():
+            mask_tiles(shard)
 
         def rows_of(i, _):
             rows = pl.ds(pl.multiple_of(i * tile, tile), tile)
@@ -172,13 +191,15 @@
         for qi in range(2):
             @pl.when(c != qi)
             def _():
-                to_sibling(2 * p + qi, p).start()
+                to_sibling(2 * p + qi, p, 1 - x).start()
+                to_sibling(2 * p + qi, p, x).start()
 
     def reduce_b(p):
         q = 2 * p + c
-        to_sibling(q, p).wait_recv()
+        to_sibling(q, p, 1 - x).wait_recv()
         acc[q, 1 - x] += sib[p, 1 - x]
         to_opposite(q, p).start()
+        to_sibling(q, p, x).wait_recv()
         acc[q, x] += sib[p, x]
 
     def reduce_c(p):
@@ -193,9 +214,9 @@
 
         lax.fori_loop(0, rows_out // BLOCK, cols, 0)
 
-    def mask_tiles():
+    def mask_tiles(shard):
         def tile(i, _):
-            r, k = i // (V.shape[1] // BLOCK), i % (V.shape[1] // BLOCK)
+            r, k = i // (R // BLOCK), shard * (R // BLOCK) + i % (R // BLOCK)
             at = (
                 pl.ds(pl.multiple_of(r * BLOCK, BLOCK), BLOCK),
                 pl.ds(pl.multiple_of(k * BLOCK, BLOCK), BLOCK),
@@ -204,7 +225,7 @@
             V[at] = V[at] * keep
             return 0
 
-        lax.fori_loop(0, (rows_out // BLOCK) * (V.shape[1] // BLOCK), tile, 0)
+        lax.fori_loop(0, (rows_out // BLOCK) * (R // BLOCK), tile, 0)
 
     def step(t, _):
         p, s = t // nz, t % nz
@@ -225,7 +246,6 @@
                     choose(q)
                 acc[...] = jnp.zeros_like(acc)
                 load_v.wait()
-                mask_tiles()
 
             each(p, s, lambda q, o: gemm(q, 2 * o + y))
 
@@ -265,7 +285,8 @@
     for q in range(Q):
         y_last(q, y).wait_send()
     for p in range(pairs):
-        to_sibling(2 * p + 1 - c, p).wait_send()
+        for h in range(2):
+            to_sibling(2 * p + 1 - c, p, h).wait_send()
         to_opposite(2 * p + c, p).wait_send()
 
 
@@ -274,12 +295,12 @@
     R, occ = amplitudes.shape
     Q, nz = NB // 2, nb // 2
     beta = max(16, R // 6 // 16 * 16)
-    chosen = jnp.take(amplitudes.reshape(R, NB, BATCH), pair_batches, axis=1).reshape(R, occ)
     dma = pltpu.SemaphoreType.DMA
     return pl.pallas_call(
         functools.partial(kernel, nz, beta),
         out_shape=jax.ShapeDtypeStruct((occ // 4, rows_out), jnp.bfloat16),
         in_specs=[
+            pl.BlockSpec(memory_space=pltpu.SMEM),
             pl.BlockSpec(memory_space=pltpu.SMEM),
             pl.BlockSpec(memory_space=pltpu.VMEM),
             pl.BlockSpec(memory_space=pl.ANY),
@@ -294,7 +315,7 @@
             dma,
             dma((Q, 2, nz)), dma((Q, 2, nz)), dma((Q, nz)), dma((Q, nz)),
             dma((Q, nz)), dma((Q, nz)), dma((Q,)), dma((Q,)),
-            dma((Q // 2,)), dma((Q // 2,)), dma((Q // 2,)), dma((Q // 2,)),
+            dma((Q // 2, 2)), dma((Q // 2, 2)), dma((Q // 2,)), dma((Q // 2,)),
         ],
         compiler_params=pltpu.CompilerParams(
             collective_id=0, has_side_effects=True, vmem_limit_bytes=56 * 2**20
@@ -304,7 +325,7 @@
             bytes_accessed=2 * rows_out * number + 2 * nb * R * occ,
             transcendentals=0,
         ),
-    )(block_mask, chosen, integrals)
+    )(block_mask, pair_batches, amplitudes, integrals)
 
 
 def solution(mesh):

time: 205 us -> 199 us (0.971)
  local copies, waits for them, and re-layouts: 9.74 us -> 1.87 us
  Pallas kernels: 193 us -> 197 us
    pallas_call x1, Pallas kernels: 193 us -> 197 us  [fused(): pl.pallas_call(functools.partial(kernel, nz, beta), out_shape=jax.ShapeDt...]
    unnamed x4 -> x1, local copies, waits for them, and re-layouts: 4.73 us -> 1.87 us
    gather x1 -> x0, local copies, waits for them, and re-layouts: 2.54 us -> none  [fused(): jnp.take(amplitudes.reshape(R, NB, BATCH), pair_batches, axis=1)]
    reshape x1 -> x0, local copies, waits for them, and re-layouts: 2.4 us -> none  [fused(): amplitudes.reshape(R, NB, BATCH)]
where the time goes in v2:
time: 199 us
  Pallas kernels  197 us (99%)
    pallas_call x1, Pallas kernels, fused(): pl.pallas_call(functools.partial(kernel, nz, beta), out_shape=jax.ShapeDt...  197 us

profile of v2, /device:TPU:1, one launch (start us, length us, event | category | flops | bytes accessed | tf_op | source)
XLA Modules:
  0.0 198.6 jit_solution(18214857819408370564)
XLA Ops:
  0.0 196.7 %shard_map.46 = bf16[256,1024]{1,0:T(8,128)(2,1)} custom-call(s32[8,64]{1,0:T(8,128)} %mask_ref.1, s32[8]{0:T(128)} %order_ref.1, bf16[1024,1024]{1,0:T(8,128)(2,1)} %amp_ref.1, bf16[1024,8192]{1,0:T(8,128)(2,1)} %int_ref.1), custom_call_target="tpu_custom_call" | custom-call | flops 17179869184 | bytes 33554432 | tf_op jit(solution)/shard_map/pallas_call | solution.py:299
  196.7 1.9 copy.6

commit v3 on v2

--- a/solution.py
+++ b/solution.py
@@ -171,7 +171,7 @@
                     def _():
                         z_part(q, o, d).start()
 
-    def each(p, s, act):
+    def each(p, s, act, low=0, high=4):
         def one(i, _):
             q, d = 2 * p + i // 2, i % 2
             o = z + s * (2 * d - 1)
@@ -181,18 +181,21 @@
                 act(q, o)
             return 0
 
-        lax.fori_loop(0, 4, one, 0)
+        lax.fori_loop(low, high, one, 0)
 
     def lagged(q, o):
         y_first(q, o, 1 - y).wait_recv()
         gemm(q, 2 * o + 1 - y)
 
+    def hand_over(p, qi):
+        @pl.when(c != qi)
+        def _():
+            to_sibling(2 * p + qi, p, 1 - x).start()
+            to_sibling(2 * p + qi, p, x).start()
+
     def reduce_a(p):
         for qi in range(2):
-            @pl.when(c != qi)
-            def _():
-                to_sibling(2 * p + qi, p, 1 - x).start()
-                to_sibling(2 * p + qi, p, x).start()
+            hand_over(p, qi)
 
     def reduce_b(p):
         q = 2 * p + c
@@ -261,9 +264,17 @@
                 act(done)
         return 0
 
-    lax.fori_loop(0, pairs * nz + LAG, step, 0)
-    for act in (reduce_a, reduce_b, reduce_c):
-        act(pairs - 1)
+    lax.fori_loop(0, pairs * nz + LAG - 1, step, 0)
+    last = pairs - 1
+    for qi in range(2):
+        each(last, nz - 1, lagged, 2 * qi, 2 * qi + 2)
+        hand_over(last, qi)
+
+        @pl.when(c == qi)
+        def _():
+            reduce_b(last)
+
+    reduce_c(last)
 
     def drain(i, _):
         q, o = i // nz, i % nz

time: 199 us -> 197 us (0.990)
  Pallas kernels: 197 us -> 195 us
where the time goes in v3:
time: 197 us
  Pallas kernels  195 us (99%)
    pallas_call x1, Pallas kernels, fused(): pl.pallas_call(functools.partial(kernel, nz, beta), out_shape=jax.ShapeDt...  195 us

profile of v3, /device:TPU:1, one launch (start us, length us, event | category | flops | bytes accessed | tf_op | source)
XLA Modules:
  0.0 197.2 jit_solution(12975536513790185318)
XLA Ops:
  0.0 195.3 %shard_map.46 = bf16[256,1024]{1,0:T(8,128)(2,1)} custom-call(s32[8,64]{1,0:T(8,128)} %mask_ref.1, s32[8]{0:T(128)} %order_ref.1, bf16[1024,1024]{1,0:T(8,128)(2,1)} %amp_ref.1, bf16[1024,8192]{1,0:T(8,128)(2,1)} %int_ref.1), custom_call_target="tpu_custom_call" | custom-call | flops 17179869184 | bytes 33554432 | tf_op jit(solution)/shard_map/pallas_call | solution.py:310
  195.3 1.9 copy.6

commit v4 on v3

--- a/solution.py
+++ b/solution.py
@@ -305,7 +305,7 @@
     rows_out, number = integrals.shape
     R, occ = amplitudes.shape
     Q, nz = NB // 2, nb // 2
-    beta = max(16, R // 6 // 16 * 16)
+    beta = max(32, R // 10 // 32 * 32)
     dma = pltpu.SemaphoreType.DMA
     return pl.pallas_call(
         functools.partial(kernel, nz, beta),

time: 197 us -> 194 us (0.985)
  the two profiles are of different devices: /device:TPU:1 before, /device:TPU:17 now
where the time goes in v4:
time: 194 us; the launch traced here: 193 us
  Pallas kernels  192 us (99%)
    pallas_call x1, Pallas kernels, fused(): pl.pallas_call(functools.partial(kernel, nz, beta), out_shape=jax.ShapeDt...  192 us

profile of v4, /device:TPU:17, one launch (start us, length us, event | category | flops | bytes accessed | tf_op | source)
XLA Modules:
  0.0 193.5 jit_solution(14563543437134372094)
XLA Ops:
  0.0 191.6 %shard_map.46 = bf16[256,1024]{1,0:T(8,128)(2,1)} custom-call(s32[8,64]{1,0:T(8,128)} %mask_ref.1, s32[8]{0:T(128)} %order_ref.1, bf16[1024,1024]{1,0:T(8,128)(2,1)} %amp_ref.1, bf16[1024,8192]{1,0:T(8,128)(2,1)} %int_ref.1), custom_call_target="tpu_custom_call" | custom-call | flops 17179869184 | bytes 33554432 | tf_op jit(solution)/shard_map/pallas_call | solution.py:310
  191.6 1.9 copy.6
